TPU v7x, 128 devices: a whole 4x4x4 slice. The times are simulated.
128 devices in a mesh: seq: 32 (over x_lo, z, y), mp: 4 (over x_hi, core).
Axes of the slice: x: 4 (x_hi: 2, x_lo: 2; x = x_hi * 2 + x_lo), y: 4, z: 4, core: 2. Of those that a mesh axis runs over, the one named last changes fastest.
Arguments:
- tokens: bfloat16 [16384, 1152], P('seq'), may hold values from -6 to 6
- grad_out: bfloat16 [16384, 1152], P('seq'), may hold values from -6 to 6
- attn_pre_gain: bfloat16 [1152], P('seq'), may hold values from 0.25 to 1.75
- w_query: bfloat16 [1152, 1024], P('seq', 'mp'), may hold values from -0.1875 to 0.1875
- query_gain: bfloat16 [256], P('seq'), may hold values from 0.25 to 1.75
- key_gain: bfloat16 [256], P('seq'), may hold values from 0.25 to 1.75
- w_keyval: bfloat16 [1152, 512], P(('seq', 'mp')), may hold values from -0.1875 to 0.1875
- w_out: bfloat16 [1024, 1152], P('mp', 'seq'), may hold values from -0.75 to 0.75
- attn_post_gain: bfloat16 [1152], P('seq'), may hold values from 0.25 to 1.75
- ffn_pre_gain: bfloat16 [1152], P('seq'), may hold values from 0.25 to 1.75
- w_gate: bfloat16 [1152, 6912], P('seq', 'mp'), may hold values from -0.1875 to 0.1875
- w_up: bfloat16 [1152, 6912], P('seq', 'mp'), may hold values from -0.1875 to 0.1875
- w_down: bfloat16 [6912, 1152], P('mp', 'seq'), may hold values from -0.078125 to 0.078125
- ffn_post_gain: bfloat16 [1152], P('seq'), may hold values from 0.25 to 1.75
Outputs:
- output: bfloat16 [16384, 1152], P('seq')
- grad_tokens: bfloat16 [16384, 1152], P('seq')
- grad_attn_pre_gain: float32 [1152], P('seq')
- grad_w_query: float32 [1152, 1024], P('seq', 'mp')
- grad_query_gain: float32 [256], P('seq')
- grad_key_gain: float32 [256], P('seq')
- grad_w_keyval: float32 [1152, 512], P(('seq', 'mp'))
- grad_w_out: float32 [1024, 1152], P('mp', 'seq')
- grad_attn_post_gain: float32 [1152], P('seq')
- grad_ffn_pre_gain: float32 [1152], P('seq')
- grad_w_gate: float32 [1152, 6912], P('seq', 'mp')
- grad_w_up: float32 [1152, 6912], P('seq', 'mp')
- grad_w_down: float32 [6912, 1152], P('mp', 'seq')
- grad_ffn_post_gain: float32 [1152], P('seq')
All inputs are finite; a program needn't handle non-finite values.
Results may differ from a plain program's by a relative error of at most 0.03.
Values may be sent and summed in bfloat16 or wider, within the bound.
No kernel may reach another device: no remote copies, remote signals or barrier semaphores. Data moves between devices by JAX's collectives and lax.ppermute only.
A program may use at most 128 MiB of HBM per device.

v0:
```python
import jax
import jax.numpy as jnp
from jax import lax
from jax.sharding import PartitionSpec as P

HD = 256
WINDOW = 512
SEQ_BLOCKS = 8


EPS = 1e-06
SCALE = 0.0625
MASKED = -1e30


def passed_along(shard, axis, by):
    devices = lax.axis_size(axis)
    pairs = [(i, i + by) for i in range(devices) if 0 <= i + by < devices]
    return lax.ppermute(shard, axis, pairs)


def rms_norm(values, gain):
    return values * lax.rsqrt(jnp.mean(values * values, axis=-1, keepdims=True) + EPS) * gain


def rotary(values, angle):
    half_width = values.shape[-1] // 2
    former = values[..., :half_width]
    latter = values[..., half_width:]
    cosine = jnp.cos(angle)
    sine = jnp.sin(angle)
    return jnp.concatenate(
        [former * cosine - latter * sine, latter * cosine + former * sine], axis=-1
    )


def gelu_tanh(values):
    return (
        0.5
        * values
        * (1.0 + jnp.tanh(0.7978845608028654 * (values + 0.044715 * values * values * values)))
    )


def gated_hidden(gate_in, up_in):
    return gelu_tanh(gate_in) * up_in


def angles(row_start, count):
    positions = (row_start + jnp.arange(count, dtype=jnp.int32)).astype(jnp.float32)
    exponent = jnp.arange(HD // 2, dtype=jnp.float32) * (-2.0 / HD)
    return positions[:, None] * jnp.power(10000.0, exponent)[None, :]


def allowed_mask(row_count, first_pos):
    row_ids = jnp.arange(row_count, dtype=jnp.int32)[:, None]
    key_ids = jnp.arange(row_count + WINDOW, dtype=jnp.int32)[None, :]
    return (key_ids > row_ids) & (key_ids <= row_ids + WINDOW) & (key_ids + first_pos >= WINDOW)


def norm_back(values, gain, incoming):
    _, pull = jax.vjp(rms_norm, values, gain)
    return pull(incoming)


def per_device(
    tokens,
    grad_out,
    attn_pre_gain,
    w_query,
    query_gain,
    key_gain,
    w_keyval,
    w_out,
    attn_post_gain,
    ffn_pre_gain,
    w_gate,
    w_up,
    w_down,
    ffn_post_gain,
):
    block_rows = tokens.shape[0]
    heads_here = w_query.shape[1] // HD
    row_count = min(block_rows, 512)
    seq_start = lax.axis_index("seq") % SEQ_BLOCKS * block_rows
    attn_params = (
        lax.all_gather(attn_pre_gain, "seq", axis=0, tiled=True),
        lax.all_gather(w_query, "seq", axis=0, tiled=True),
        lax.all_gather(query_gain, "seq", axis=0, tiled=True),
        lax.all_gather(key_gain, "seq", axis=0, tiled=True),
        lax.all_gather(w_out, "seq", axis=1, tiled=True),
        lax.all_gather(attn_post_gain, "seq", axis=0, tiled=True),
    )
    pre_gain = attn_params[0].astype(jnp.float32)
    query_weight = attn_params[1]
    qnorm_gain = attn_params[2].astype(jnp.float32)
    knorm_gain = attn_params[3].astype(jnp.float32)
    out_weight = attn_params[4]
    post_gain = attn_params[5].astype(jnp.float32)
    keyval_weight = lax.all_gather(w_keyval, ("seq", "mp"), axis=0, tiled=True)
    inputs = tokens.astype(jnp.float32)
    normed_x = rms_norm(inputs, pre_gain).astype(jnp.bfloat16)
    query_raw = jnp.dot(normed_x, query_weight, preferred_element_type=jnp.float32).reshape(
        block_rows, heads_here, HD
    )
    keyval_raw = jnp.dot(normed_x, keyval_weight, preferred_element_type=jnp.float32)
    key_raw = keyval_raw[:, :HD]
    angle = angles(seq_start, block_rows)
    query = rotary(rms_norm(query_raw, qnorm_gain), angle[:, None, :]).astype(jnp.bfloat16)
    key_rot = rotary(rms_norm(key_raw, knorm_gain), angle).astype(jnp.bfloat16)
    value_low = keyval_raw[:, HD:].astype(jnp.bfloat16)
    halo_key, halo_value = passed_along((key_rot, value_low), "seq", 1)
    keys_all = jnp.concatenate([halo_key, key_rot], axis=0)
    values_all = jnp.concatenate([halo_value, value_low], axis=0)
    part_index = 0
    row_start = part_index * row_count
    score = jnp.einsum("rhd,kd->hrk", query, keys_all, preferred_element_type=jnp.float32) * SCALE
    score = jnp.where(allowed_mask(row_count, seq_start + row_start)[None], score, MASKED)
    peak = jnp.max(score, axis=-1, keepdims=True)
    weight = jnp.exp(score - peak)
    weight_sum = jnp.sum(weight, axis=-1, keepdims=True)
    prob_low = (weight / weight_sum).astype(jnp.bfloat16)
    out_parts = jnp.einsum("hrk,kd->rhd", prob_low, values_all, preferred_element_type=jnp.float32)
    lse_parts = [peak + jnp.log(weight_sum)]
    attended = out_parts.astype(jnp.bfloat16).reshape(block_rows, heads_here * HD)
    branch_part = jnp.dot(attended, out_weight, preferred_element_type=jnp.float32)
    branch = lax.psum(branch_part, "mp")
    middle = inputs + rms_norm(branch, post_gain)
    ffn_params = (
        lax.all_gather(ffn_pre_gain, "seq", axis=0, tiled=True),
        lax.all_gather(w_gate, "seq", axis=0, tiled=True),
        lax.all_gather(w_up, "seq", axis=0, tiled=True),
        lax.all_gather(w_down, "seq", axis=1, tiled=True),
        lax.all_gather(ffn_post_gain, "seq", axis=0, tiled=True),
    )
    ffn_pre = ffn_params[0].astype(jnp.float32)
    ffn_post = ffn_params[4].astype(jnp.float32)
    normed_mid = rms_norm(middle, ffn_pre).astype(jnp.bfloat16)
    gate = jnp.dot(normed_mid, ffn_params[1], preferred_element_type=jnp.float32)
    up_proj = jnp.dot(normed_mid, ffn_params[2], preferred_element_type=jnp.float32)
    hidden = gated_hidden(gate, up_proj).astype(jnp.bfloat16)
    ffn_out = lax.psum(jnp.dot(hidden, ffn_params[3], preferred_element_type=jnp.float32), "mp")
    output = (middle + rms_norm(ffn_out, ffn_post)).astype(jnp.bfloat16)
    ffn_params = (
        lax.all_gather(ffn_pre_gain, "seq", axis=0, tiled=True),
        lax.all_gather(w_gate, "seq", axis=0, tiled=True),
        lax.all_gather(w_up, "seq", axis=0, tiled=True),
        lax.all_gather(w_down, "seq", axis=1, tiled=True),
        lax.all_gather(ffn_post_gain, "seq", axis=0, tiled=True),
    )
    gate_weight = ffn_params[1]
    up_weight = ffn_params[2]
    down_weight = ffn_params[3]
    grad_y = grad_out.astype(jnp.float32)
    grad_ffn, grad_ffn_post = norm_back(ffn_out, ffn_post, grad_y)
    grad_ffn_low = grad_ffn.astype(jnp.bfloat16)
    grad_down = jnp.einsum("tf,td->fd", hidden, grad_ffn_low, preferred_element_type=jnp.float32)
    grad_hidden = jnp.einsum(
        "td,fd->tf", grad_ffn_low, down_weight, preferred_element_type=jnp.float32
    )
    _, gate_pull = jax.vjp(gated_hidden, gate, up_proj)
    grad_gate, grad_up = gate_pull(grad_hidden)
    grad_gate_low = grad_gate.astype(jnp.bfloat16)
    grad_up_low = grad_up.astype(jnp.bfloat16)
    grad_w_gate = jnp.einsum(
        "td,tf->df", normed_mid, grad_gate_low, preferred_element_type=jnp.float32
    )
    grad_w_up = jnp.einsum("td,tf->df", normed_mid, grad_up_low, preferred_element_type=jnp.float32)
    normed_part = jnp.einsum(
        "tf,df->td", grad_gate_low, gate_weight, preferred_element_type=jnp.float32
    )
    normed_part = normed_part + jnp.einsum(
        "tf,df->td", grad_up_low, up_weight, preferred_element_type=jnp.float32
    )
    grad_normed_mid = lax.psum(normed_part, "mp")
    grad_mid_norm, grad_ffn_pre = norm_back(middle, ffn_pre, grad_normed_mid)
    grad_middle = grad_y + grad_mid_norm
    ffn_grads = (
        lax.psum_scatter(
            grad_ffn_pre.astype(jnp.bfloat16), "seq", scatter_dimension=0, tiled=True
        ).astype(jnp.float32),
        lax.psum_scatter(
            grad_w_gate.astype(jnp.bfloat16), "seq", scatter_dimension=0, tiled=True
        ).astype(jnp.float32),
        lax.psum_scatter(
            grad_w_up.astype(jnp.bfloat16), "seq", scatter_dimension=0, tiled=True
        ).astype(jnp.float32),
        lax.psum_scatter(
            grad_down.astype(jnp.bfloat16), "seq", scatter_dimension=1, tiled=True
        ).astype(jnp.float32),
        lax.psum_scatter(
            grad_ffn_post.astype(jnp.bfloat16), "seq", scatter_dimension=0, tiled=True
        ).astype(jnp.float32),
    )
    grad_branch, grad_post = norm_back(branch, post_gain, grad_middle)
    grad_branch_low = grad_branch.astype(jnp.bfloat16)
    grad_w_out = jnp.einsum(
        "ta,td->ad", attended, grad_branch_low, preferred_element_type=jnp.float32
    )
    grad_att = jnp.einsum(
        "td,ad->ta", grad_branch_low, out_weight, preferred_element_type=jnp.float32
    )
    grad_att = grad_att.astype(jnp.bfloat16).reshape(block_rows, heads_here, HD)
    grad_keys = jnp.zeros((WINDOW + block_rows, HD), jnp.float32)
    grad_values = jnp.zeros((WINDOW + block_rows, HD), jnp.float32)
    part_index = 0
    row_start = part_index * row_count
    mask_here = allowed_mask(row_count, seq_start + row_start)[None]
    score = jnp.einsum("rhd,kd->hrk", query, keys_all, preferred_element_type=jnp.float32) * SCALE
    prob_full = jnp.where(mask_here, jnp.exp(score - lse_parts[part_index]), 0.0)
    prob_low = prob_full.astype(jnp.bfloat16)
    grad_prob = jnp.einsum("rhd,kd->hrk", grad_att, values_all, preferred_element_type=jnp.float32)
    delta = jnp.sum(prob_full * grad_prob, axis=-1, keepdims=True)
    grad_score = (prob_full * (grad_prob - delta)).astype(jnp.bfloat16)
    grad_query_parts = (
        jnp.einsum("hrk,kd->rhd", grad_score, keys_all, preferred_element_type=jnp.float32) * SCALE
    )
    key_term = (
        jnp.einsum("hrk,rhd->kd", grad_score, query, preferred_element_type=jnp.float32) * SCALE
    )
    value_term = jnp.einsum("hrk,rhd->kd", prob_low, grad_att, preferred_element_type=jnp.float32)
    grad_keys = grad_keys.at[row_start : row_start + row_count + WINDOW].add(key_term)
    grad_values = grad_values.at[row_start : row_start + row_count + WINDOW].add(value_term)
    back_keys, back_values = (
        passed_along(grad_keys[:WINDOW].astype(jnp.bfloat16), "seq", -1).astype(jnp.float32),
        passed_along(grad_values[:WINDOW].astype(jnp.bfloat16), "seq", -1).astype(jnp.float32),
    )
    own_keys = grad_keys[WINDOW:].at[block_rows - WINDOW :].add(back_keys)
    own_values = grad_values[WINDOW:].at[block_rows - WINDOW :].add(back_values)
    key_share, value_share = (
        lax.psum_scatter(
            own_keys.astype(jnp.bfloat16), "mp", scatter_dimension=0, tiled=True
        ).astype(jnp.float32),
        lax.psum_scatter(
            own_values.astype(jnp.bfloat16), "mp", scatter_dimension=0, tiled=True
        ).astype(jnp.float32),
    )
    share_rows = block_rows // lax.axis_size("mp")
    share_start = lax.axis_index("mp") * share_rows
    key_raw_share = lax.dynamic_slice_in_dim(key_raw, share_start, share_rows, 0)
    angle_share = lax.dynamic_slice_in_dim(angle, share_start, share_rows, 0)

    def key_path(raw_values, gain_in):
        return rotary(rms_norm(raw_values, gain_in), angle_share)

    _, key_pull = jax.vjp(key_path, key_raw_share, knorm_gain)
    grad_key_raw, grad_key_gain = key_pull(key_share)
    grad_keyval_low = jnp.concatenate([grad_key_raw, value_share], axis=1).astype(jnp.bfloat16)
    normed_share = lax.dynamic_slice_in_dim(normed_x, share_start, share_rows, 0)
    grad_w_keyval = jnp.einsum(
        "td,tc->dc", normed_share, grad_keyval_low, preferred_element_type=jnp.float32
    )

    def query_path(raw_values, gain_in):
        return rotary(rms_norm(raw_values, gain_in), angle[:, None, :])

    _, query_pull = jax.vjp(query_path, query_raw, qnorm_gain)
    grad_query_raw, grad_query_gain = query_pull(grad_query_parts)
    grad_query_low = grad_query_raw.reshape(block_rows, heads_here * HD).astype(jnp.bfloat16)
    grad_w_query = jnp.einsum(
        "td,tq->dq", normed_x, grad_query_low, preferred_element_type=jnp.float32
    )
    normed_grad = jnp.einsum(
        "tq,dq->td", grad_query_low, query_weight, preferred_element_type=jnp.float32
    )
    keyval_term = jnp.einsum(
        "tc,dc->td", grad_keyval_low, keyval_weight, preferred_element_type=jnp.float32
    )
    normed_grad = lax.dynamic_update_slice_in_dim(
        normed_grad,
        lax.dynamic_slice_in_dim(normed_grad, share_start, share_rows, 0) + keyval_term,
        share_start,
        0,
    )
    normed_grad, grad_query_gain, grad_key_gain = (
        lax.psum(normed_grad.astype(jnp.bfloat16), "mp").astype(jnp.float32),
        lax.psum(grad_query_gain.astype(jnp.bfloat16), "mp").astype(jnp.float32),
        lax.psum(grad_key_gain.astype(jnp.bfloat16), "mp").astype(jnp.float32),
    )
    grad_x_norm, grad_pre = norm_back(inputs, pre_gain, normed_grad)
    grad_tokens = (grad_middle + grad_x_norm).astype(jnp.bfloat16)
    attn_grads = (
        lax.psum_scatter(
            grad_pre.astype(jnp.bfloat16), "seq", scatter_dimension=0, tiled=True
        ).astype(jnp.float32),
        lax.psum_scatter(
            grad_w_query.astype(jnp.bfloat16), "seq", scatter_dimension=0, tiled=True
        ).astype(jnp.float32),
        lax.psum_scatter(
            grad_query_gain.astype(jnp.bfloat16), "seq", scatter_dimension=0, tiled=True
        ).astype(jnp.float32),
        lax.psum_scatter(
            grad_key_gain.astype(jnp.bfloat16), "seq", scatter_dimension=0, tiled=True
        ).astype(jnp.float32),
        lax.psum_scatter(
            grad_w_out.astype(jnp.bfloat16), "seq", scatter_dimension=1, tiled=True
        ).astype(jnp.float32),
        lax.psum_scatter(
            grad_post.astype(jnp.bfloat16), "seq", scatter_dimension=0, tiled=True
        ).astype(jnp.float32),
    )
    keyval_grads = lax.psum_scatter(grad_w_keyval, ("seq", "mp"), scatter_dimension=0, tiled=True)
    return (
        output,
        grad_tokens,
        attn_grads[0],
        attn_grads[1],
        attn_grads[2],
        attn_grads[3],
        keyval_grads,
        attn_grads[4],
        attn_grads[5],
        ffn_grads[0],
        ffn_grads[1],
        ffn_grads[2],
        ffn_grads[3],
        ffn_grads[4],
    )


def solution(mesh):
    placed = (
        P("seq", None),
        P("seq", None),
        P("seq"),
        P("seq", "mp"),
        P("seq"),
        P("seq"),
        P(("seq", "mp"), None),
        P("mp", "seq"),
        P("seq"),
        P("seq"),
        P("seq", "mp"),
        P("seq", "mp"),
        P("mp", "seq"),
        P("seq"),
    )
    return jax.shard_map(
        per_device,
        mesh=mesh,
        in_specs=placed,
        out_specs=(
            P("seq", None),
            P("seq", None),
            P("seq"),
            P("seq", "mp"),
            P("seq"),
            P("seq"),
            P(("seq", "mp"), None),
            P("mp", "seq"),
            P("seq"),
            P("seq"),
            P("seq", "mp"),
            P("seq", "mp"),
            P("mp", "seq"),
            P("seq"),
        ),
        check_vma=False,
    )
```

profile of v0, /device:TPU:1, one launch (start us, length us, event | category | flops | bytes accessed | tf_op | source)
XLA Modules:
  0.0 1642.6 jit_solution(14559290860166623194)
XLA Ops:
  16.6 132.5 %all-reduce.28 = (bf16[256]{0:T(256)(128)(2,1)S(1)}, bf16[1152]{0:T(1024)(128)(2,1)S(1)}, bf16[256]{0:T(256)(128)(2,1)S(1)}, bf16[1152]{0:T(1024)(128)(2,1)}, bf...) all-reduce(bf16[256]{0:T(256)(128)(2,1)S(1)} %dynamic-update-slice.9, ...), channel_id=1, replica_groups=mesh['seq'=32,'mp'=4] {'seq'}, use_global_device_ids=true, to_apply=%add.5 | all-reduce | flops 5120 | bytes 20480
  149.1 65.5 %all-gather.1 = bf16[32,36,256]{2,1,0:T(8,128)(2,1)S(1)} all-gather(bf16[1,36,256]{2,1,0:T(8,128)(2,1)} %bitcast.142), channel_id=1, replica_groups=mesh['seq'=32,'mp'=4] {'seq'}, dimensions={0}, use_global_device_ids=true | all-gather | bytes 608256 | tf_op jit(solution)/shard_map/all_gather | solution.py:88
  218.9 71.7 %all-gather.2 = bf16[32,36,256]{2,1,0:T(8,128)(2,1)} all-gather(bf16[1,36,256]{2,1,0:T(8,128)(2,1)S(1)} %bitcast.143), channel_id=1, replica_groups=mesh['seq'=32,'mp'=4] {'seq'}, dimensions={0}, use_global_device_ids=true | all-gather | bytes 608256 | tf_op jit(solution)/shard_map/all_gather | solution.py:91
  314.4 129.4 %all-reduce.37.cloned.1.call-done = f32[512,1152]{1,0:T(8,128)} async-done(((f32[512,1152]{1,0:T(8,128)}), f32[512,1152]{1,0:T(8,128)}) %all-reduce.37.cloned.1.call-update) | async-done | bytes 2359312 | tf_op jit(solution)/shard_map/psum | solution.py:127
  449.6 83.2 %all-gather.13.cloned.1.call-done = bf16[32,36,1728]{2,1,0:T(8,128)(2,1)} async-done(((bf16[1,36,1728]{2,1,0:T(8,128)(2,1)}), bf16[32,36,1728]{2,1,0:T(8,128)(2,1)}) %all-gather.13.cloned.1.call-update) | async-done | bytes 3981328 | tf_op jit(solution)/shard_map/all_gather | solution.py:131
  532.8 7.3 reshape.564
  540.1 152.6 %all-gather.15.cloned.1.call-done = bf16[32,36,1728]{2,1,0:T(8,128)(2,1)} async-done(((bf16[1,36,1728]{2,1,0:T(8,128)(2,1)}), bf16[32,36,1728]{2,1,0:T(8,128)(2,1)}) %all-gather.15.cloned.1.call-update) | async-done | bytes 3981328 | tf_op jit(solution)/shard_map/all_gather | solution.py:132
  692.7 7.3 reshape.566
  712.8 141.0 %all-gather.17.cloned.1.call-done = bf16[32,36,1728]{2,1,0:T(8,128)(2,1)} async-done(((bf16[1,36,1728]{2,1,0:T(8,128)(2,1)}), bf16[32,36,1728]{2,1,0:T(8,128)(2,1)}) %all-gather.17.cloned.1.call-update) | async-done | bytes 3981328 | tf_op jit(solution)/shard_map/all_gather | solution.py:133
  853.8 7.3 reshape.568
  861.1 6.8 fusion.94
  869.5 83.1 %all-reduce.39.cloned.1.call-done = f32[512,1152]{1,0:T(8,128)} async-done(((f32[512,1152]{1,0:T(8,128)}), f32[512,1152]{1,0:T(8,128)}) %all-reduce.39.cloned.1.call-update) | async-done | bytes 2359312 | tf_op jit(solution)/shard_map/psum | solution.py:142
  961.8 7.9 multiply_convert_fusion
  995.5 44.6 %all-reduce.41.cloned.1.call-done = f32[512,1152]{1,0:T(8,128)} async-done(((f32[512,1152]{1,0:T(8,128)}), f32[512,1152]{1,0:T(8,128)}) %all-reduce.41.cloned.1.call-update) | async-done | bytes 2359312 | tf_op jit(solution)/shard_map/psum | solution.py:175
  1062.8 11.3 collective-permute-done.2
  1079.7 25.2 %reduce-scatter.17.cloned.1.call-done = bf16[128,256]{1,0:T(8,128)(2,1)} async-done(((bf16[512,256]{1,0:T(8,128)(2,1)}), bf16[128,256]{1,0:T(8,128)(2,1)}) %reduce-scatter.17.cloned.1.call-update) | async-done | bytes 65552
  1112.4 22.2 %reduce-scatter.19.cloned.1.call-done = bf16[128,256]{1,0:T(8,128)(2,1)} async-done(((bf16[512,256]{1,0:T(8,128)(2,1)}), bf16[128,256]{1,0:T(8,128)(2,1)}) %reduce-scatter.19.cloned.1.call-update) | async-done | bytes 65552
  1141.6 189.6 %fusion.88 = (bf16[40,256]{1,0:T(8,128)(2,1)}, bf16[256,40]{0,1:T(8,128)(2,1)}, bf16[40,1728]{1,0:T(8,128)(2,1)}, bf16[40,1728]{1,0:T(8,128)(2,1)}, bf16[1728,40]{0,1:T(8,128)(2,1)}) fusion(bf16[1152,256]{1,0:T(8,128)(2,1)S(1)} %copy-done.24, bf16[256,1152]{0,1:T(8,128)(2,1)S(1)} %copy-done.25, bf16[1152,1728]{1,0:T(8,128)(2,1)} %convolution_convert_fusion.2, ...), kind=kCustom, calls=%all-reduce-scatter.5 | all-reduce-scatter fusion | flops 7290881 | bytes 13579776
  1367.3 8.7 collective-permute-start.10
  1386.6 6.9 collective-permute-start.17
  1423.2 7.2 concatenate.48
  1430.5 7.8 concatenate.49
  1445.7 130.0 %all-reduce.27 = (bf16[1152]{0:T(1024)(128)(2,1)}, bf16[256]{0:T(256)(128)(2,1)}, bf16[256]{0:T(256)(128)(2,1)}, bf16[1152]{0:T(1024)(128)(2,1)}, bf16[1152]{0:T(1024)(128)(2,1)}, /*index=5*/bf16[1152]{0:T(1024)(128)(2,1)}) all-reduce(bf16[1152]{0:T(1024)(128)(2,1)} %get-tuple-element.100, ...), channel_id=4, replica_groups=mesh['seq'=32,'mp'=4] {'seq'}, use_global_device_ids=true, to_apply=%region_23.24.clone | all-reduce | flops 5120 | bytes 20480
  1579.8 44.8 %all-reduce.29 = (bf16[8]{0:T(256)(128)(2,1)}, bf16[8]{0:T(256)(128)(2,1)}) all-reduce(bf16[8]{0:T(256)(128)(2,1)} %dynamic-slice.31, bf16[8]{0:T(256)(128)(2,1)} %dynamic-slice.33), channel_id=1, replica_groups=mesh['seq'=32,'mp'=4] {'mp'}, use_global_device_ids=true, to_apply=%region_26.27 | all-reduce | flops 16 | bytes 64 | tf_op jit(solution)/shard_map/psum | solution.py:277
  (391 shorter events, 227.7 us)
Async XLA Ops:
  8.0 282.6 %all-gather.11.cloned.1.call-start = ((), (), s32[]{:S(2)}) async-start(), calls=%async_computation.6 | async-start | bytes 2113536 | tf_op jit(solution)/shard_map/all_gather | solution.py:100
  8.8 435.0 %all-reduce.37.cloned.1.call-start = ((), (), s32[]{:S(2)}) async-start(), calls=%async_computation.2 | async-start | bytes 4718592 | tf_op jit(solution)/shard_map/psum | solution.py:127
  311.5 221.3 %all-gather.13.cloned.1.call-start = ((), (), s32[]{:S(2)}) async-start(), calls=%async_computation.7 | async-start | bytes 4730880 | tf_op jit(solution)/shard_map/all_gather | solution.py:131
  312.1 380.6 %all-gather.15.cloned.1.call-start = ((), (), s32[]{:S(2)}) async-start(), calls=%async_computation.8 | async-start | bytes 4730880 | tf_op jit(solution)/shard_map/all_gather | solution.py:132
  312.7 541.2 %all-gather.17.cloned.1.call-start = ((), (), s32[]{:S(2)}) async-start(), calls=%async_computation.9 | async-start | bytes 4730880 | tf_op jit(solution)/shard_map/all_gather | solution.py:133
  313.2 639.4 %all-reduce.39.cloned.1.call-start = ((), (), s32[]{:S(2)}) async-start(), calls=%async_computation.3 | async-start | bytes 4718592 | tf_op jit(solution)/shard_map/psum | solution.py:142
  868.0 172.1 %all-reduce.41.cloned.1.call-start = ((), (), s32[]{:S(2)}) async-start(), calls=%async_computation.4 | async-start | bytes 4718592 | tf_op jit(solution)/shard_map/psum | solution.py:175
  977.3 127.6 %reduce-scatter.17.cloned.1.call-start = ((), (), s32[]{:S(2)}) async-start(), calls=%async_computation.10 | async-start | bytes 327680
  1058.8 19.0 %collective-permute-start.3 = (bf16[512,256]{1,0:T(8,128)(2,1)}, bf16[512,256]{1,0:T(8,128)(2,1)}, u32[]{:S(2)}, u32[]{:S(2)}) collective-permute-start(bf16[512,256]{1,0:T(8,128)(2,1)} %slice.143), channel_id=1, source_target_pairs={{4,0},{8,4},{12,8},{16,12},{20,16},{24,20},{28,24},{32,28},{36,32}... | collective-permute-start | bytes 786440 | tf_op jit(solution)/shard_map/ppermute | solution.py:19
  1074.9 59.7 %reduce-scatter.19.cloned.1.call-start = ((), (), s32[]{:S(2)}) async-start(), calls=%async_computation.11 | async-start | bytes 327680
  1079.7 363.0 %all-reduce.43.cloned.1.call-start = ((), (), s32[]{:S(2)}) async-start(), calls=%async_computation.5 | async-start | bytes 2359296 | tf_op jit(solution)/shard_map/psum | solution.py:276
  1141.6 491.6 %all-reduce.45.cloned.1.call-start = ((), (), s32[]{:S(2)}) async-start(), calls=%async_computation.12 | async-start | bytes 4718592
  1332.0 22.4 %collective-permute-start.15 = (bf16[4,1728]{1,0:T(4,128)(2,1)S(1)}, bf16[4,1728]{1,0:T(4,128)(2,1)S(1)}, u32[]{:S(2)}, u32[]{:S(2)}) collective-permute-start(bf16[4,1728]{1,0:T(4,128)(2,1)S(1)} %slice.113), channel_id=1, source_target_pairs={{0,16},{4,20},{8,24},{12,28},{16,32},{20,36},{24,40},{28,44},{32,4... | collective-permute-start | bytes 41480
  1334.1 21.7 %collective-permute-start.19 = (bf16[4,1728]{1,0:T(4,128)(2,1)S(1)}, bf16[4,1728]{1,0:T(4,128)(2,1)S(1)}, u32[]{:S(2)}, u32[]{:S(2)}) collective-permute-start(bf16[4,1728]{1,0:T(4,128)(2,1)S(1)} %slice.114), channel_id=1, source_target_pairs={{0,16},{4,20},{8,24},{12,28},{16,32},{20,36},{24,40},{28,44},{32,4... | collective-permute-start | bytes 41480
  1335.4 25.3 %collective-permute-start.6 = (bf16[40,256]{1,0:T(8,128)(2,1)}, bf16[40,256]{1,0:T(8,128)(2,1)S(1)}, u32[]{:S(2)}, u32[]{:S(2)}) collective-permute-start(bf16[40,256]{1,0:T(8,128)(2,1)} %get-tuple-element.125), channel_id=1, source_target_pairs={{0,12},{4,16},{8,20},{12,24},{16,28},{20,32},{24,36},{28,40},{32,4... | collective-permute-start | bytes 61448
  1347.9 50.2 %collective-permute-start.14 = (bf16[40,1728]{1,0:T(8,128)(2,1)}, bf16[40,1728]{1,0:T(8,128)(2,1)S(1)}, u32[]{:S(2)}, u32[]{:S(2)}) collective-permute-start(bf16[40,1728]{1,0:T(8,128)(2,1)} %get-tuple-element.127), channel_id=1, source_target_pairs={{0,12},{4,16},{8,20},{12,24},{16,28},{20,32},{24,36},{28,40},{32,4... | collective-permute-start | bytes 414728
  1349.2 54.2 %collective-permute-start.13 = (bf16[40,1728]{1,0:T(8,128)(2,1)}, bf16[40,1728]{1,0:T(8,128)(2,1)S(1)}, u32[]{:S(2)}, u32[]{:S(2)}) collective-permute-start(bf16[40,1728]{1,0:T(8,128)(2,1)} %get-tuple-element.127), channel_id=1, source_target_pairs={{0,8},{4,12},{8,16},{12,20},{16,24},{20,28},{24,32},{28,36},{32,40... | collective-permute-start | bytes 414728
  1354.4 54.4 %collective-permute-start.12 = (bf16[40,1728]{1,0:T(8,128)(2,1)}, bf16[40,1728]{1,0:T(8,128)(2,1)S(1)}, u32[]{:S(2)}, u32[]{:S(2)}) collective-permute-start(bf16[40,1728]{1,0:T(8,128)(2,1)} %get-tuple-element.127), channel_id=1, source_target_pairs={{0,4},{4,8},{8,12},{12,16},{16,20},{20,24},{24,28},{28,32},{32,36}... | collective-permute-start | bytes 414728
  1355.7 57.9 %collective-permute-start.18 = (bf16[40,1728]{1,0:T(8,128)(2,1)}, bf16[40,1728]{1,0:T(8,128)(2,1)S(1)}, u32[]{:S(2)}, u32[]{:S(2)}) collective-permute-start(bf16[40,1728]{1,0:T(8,128)(2,1)} %get-tuple-element.128), channel_id=1, source_target_pairs={{0,12},{4,16},{8,20},{12,24},{16,28},{20,32},{24,36},{28,40},{32,4... | collective-permute-start | bytes 414728
  1386.6 30.9 %collective-permute-start.17 = (bf16[40,1728]{1,0:T(8,128)(2,1)}, bf16[40,1728]{1,0:T(8,128)(2,1)S(1)}, u32[]{:S(2)}, u32[]{:S(2)}) collective-permute-start(bf16[40,1728]{1,0:T(8,128)(2,1)} %get-tuple-element.128), channel_id=1, source_target_pairs={{0,8},{4,12},{8,16},{12,20},{16,24},{20,28},{24,32},{28,36},{32,40... | collective-permute-start | bytes 414728
  1398.0 25.2 %collective-permute-start.16 = (bf16[40,1728]{1,0:T(8,128)(2,1)}, bf16[40,1728]{1,0:T(8,128)(2,1)}, u32[]{:S(2)}, u32[]{:S(2)}) collective-permute-start(bf16[40,1728]{1,0:T(8,128)(2,1)} %get-tuple-element.128), channel_id=1, source_target_pairs={{0,4},{4,8},{8,12},{12,16},{16,20},{20,24},{24,28},{28,32},{32,36}... | collective-permute-start | bytes 414728
  1403.4 27.1 %collective-permute-start.22 = (bf16[1728,40]{0,1:T(8,128)(2,1)}, bf16[1728,40]{0,1:T(8,128)(2,1)}, u32[]{:S(2)}, u32[]{:S(2)}) collective-permute-start(bf16[1728,40]{0,1:T(8,128)(2,1)} %get-tuple-element.129), channel_id=1, source_target_pairs={{0,12},{4,16},{8,20},{12,24},{16,28},{20,32},{24,36},{28,40},{32,4... | collective-permute-start | bytes 414728
  1408.8 21.6 %collective-permute-start.21 = (bf16[1728,40]{0,1:T(8,128)(2,1)}, bf16[1728,40]{0,1:T(8,128)(2,1)}, u32[]{:S(2)}, u32[]{:S(2)}) collective-permute-start(bf16[1728,40]{0,1:T(8,128)(2,1)} %get-tuple-element.129), channel_id=1, source_target_pairs={{0,8},{4,12},{8,16},{12,20},{16,24},{20,28},{24,32},{28,36},{32,40... | collective-permute-start | bytes 414728
  1413.7 16.8 %collective-permute-start.20 = (bf16[1728,40]{0,1:T(8,128)(2,1)}, bf16[1728,40]{0,1:T(8,128)(2,1)}, u32[]{:S(2)}, u32[]{:S(2)}) collective-permute-start(bf16[1728,40]{0,1:T(8,128)(2,1)} %get-tuple-element.129), channel_id=1, source_target_pairs={{0,4},{4,8},{8,12},{12,16},{16,20},{20,24},{24,28},{28,32},{32,36}... | collective-permute-start | bytes 414728
  (112 other events, 1669.5 us)
Sparse Core Ops, SparseCore 0:
  10.6 197.6 all-gather.10
  311.6 132.1 all-reduce.36
  868.1 84.4 all-reduce.38
  977.4 62.5 all-reduce.40
  1075.0 29.9 reduce-scatter.16
  1108.1 26.3 reduce-scatter.18
  1141.7 62.8 all-reduce.42
  1442.8 165.2 all-reduce.44
Sparse Core Ops, SparseCore 1:
  313.6 219.1 all-gather.12
  534.3 158.3 all-gather.14
  694.2 159.5 all-gather.16
where the time goes:
time: 1650 us; the launch traced here: 1640 us
  waiting for transfers between devices  703 us (43%)
  blocking collectives  634 us (38%)
  starting transfers between devices  80.5 us (5%)
  local copies, waits for them, and re-layouts  75.8 us (5%)
  matrix products  66.5 us (4%)
  other arithmetic  62.3 us (4%)
  between operations  21 us (1%)
    unnamed x3, blocking collectives  452 us
    all_gather x1, waiting for transfers between devices, per_device(): lax.all_gather(w_up, 'seq', axis=0, tiled=True)  153 us
    all_gather x1, waiting for transfers between devices, per_device(): lax.all_gather(w_down, 'seq', axis=1, tiled=True)  141 us
    psum x1, waiting for transfers between devices, per_device(): branch = lax.psum(branch_part, 'mp')  129 us
    all_gather x1, waiting for transfers between devices, per_device(): lax.all_gather(w_gate, 'seq', axis=0, tiled=True)  83.2 us
    psum x1, waiting for transfers between devices, per_device(): lax.psum(jnp.dot(hidden, ffn_params[3], preferred_element_type=jnp.float3...  83.1 us
    unnamed x236, local copies, waits for them, and re-layouts  73.9 us
    unnamed x23, starting transfers between devices  73.4 us
  transfers between devices with their start and end apart: 35, of which 15 were waited for; matrix products, arithmetic and copies ran while one was open for 19% of the time, Pallas kernels for 0%

commit v1 on v0

v1 whole, which is shorter than its diff:
```python
import jax
import jax.numpy as jnp
from jax import lax
from jax.sharding import PartitionSpec as P

D = 1152
HD = 256
WINDOW = 512
SEQ_BLOCKS = 8
ROWS = 128
KEYS = ROWS + WINDOW
EPS = 1e-06
SCALE = 0.0625
MASKED = -1e30
SIZES = {"xl": 2, "z": 4, "y": 4, "xh": 2, "c": 2}
CUT = 896

bf16 = jnp.bfloat16
f32 = jnp.float32


def coords(n):
    mp, s = n % 4, n // 4
    return {"xl": s // 16, "z": s // 4 % 4, "y": s % 4, "xh": mp // 2, "c": mp % 2}


def flat(at):
    return ((at["xl"] * 4 + at["z"]) * 4 + at["y"]) * 4 + at["xh"] * 2 + at["c"]


def fetch(x, **delta):
    pairs = []
    for n in range(128):
        at = coords(n)
        for axis, by in delta.items():
            at[axis] = (at[axis] + by) % SIZES[axis]
        pairs.append((flat(at), n))
    return lax.ppermute(x, ("seq", "mp"), pairs)


def fetch_line(x, by):
    pairs = [(n + by, n) for n in range(128) if 0 <= n + by < 128]
    return lax.ppermute(x, ("seq", "mp"), pairs)


def gather_small(x, axis):
    return [x] + [fetch(x, **{axis: k}) for k in (1, 2, 3)]


def gather_big(x, axis):
    one = fetch(x, **{axis: 1})
    three = fetch(x, **{axis: 3})
    two = [fetch(one[:2], **{axis: 1}), fetch(three[2:], **{axis: 3})]
    return [x, one, jnp.concatenate(two, axis=0), three]


def gather_grid(x, route, big):
    first, second = ("z", "y") if route == 0 else ("y", "z")
    line = jnp.stack(gather_small(x, first))
    parts = (gather_big if big else gather_small)(line, second)
    return jnp.stack(parts, axis=1 if route == 0 else 0).reshape(D, x.shape[-1])


def add(*terms):
    total = terms[0].astype(f32)
    for term in terms[1:]:
        total = total + term.astype(f32)
    return total


def scatter_small(blocks, axis):
    return add(blocks[0], *[fetch(blocks[k], **{axis: 4 - k}) for k in (1, 2, 3)])


def scatter_big(blocks, axis):
    up = fetch(blocks[2][:2], **{axis: 3})
    down = fetch(blocks[2][2:], **{axis: 1})
    one = jnp.concatenate([add(blocks[1][:2], up).astype(bf16), blocks[1][2:]], axis=0)
    three = jnp.concatenate([blocks[3][:2], add(blocks[3][2:], down).astype(bf16)], axis=0)
    return add(blocks[0], fetch(one, **{axis: 3}), fetch(three, **{axis: 1}))


def scatter_grid(x, route, big):
    first, second = ("z", "y") if route == 0 else ("y", "z")
    grid = x.reshape(4, 4, 72, x.shape[-1])
    blocks = [grid[:, k] if route == 0 else grid[k] for k in range(4)]
    line = (scatter_big if big else scatter_small)(blocks, second).astype(bf16)
    return scatter_small([line[k] for k in range(4)], first)


def gather_rows(x):
    core = fetch(x, c=1)
    far = fetch(x, xh=1)
    return jnp.concatenate([x, core, far, fetch(far, c=1)], axis=0)


def scatter_rows(x):
    got = [fetch(x[ROWS : 2 * ROWS], c=1), fetch(x[3 * ROWS :], c=1)]
    far = add(x[2 * ROWS : 3 * ROWS], got[1]).astype(bf16)
    return add(x[:ROWS], got[0], fetch(far, xh=1))


def in_order(rows, xh, c):
    grid = rows.reshape(2, 2, ROWS, rows.shape[-1])
    grid = jnp.where(xh == 0, grid, grid[::-1])
    return jnp.where(c == 0, grid, grid[:, ::-1]).reshape(rows.shape)


def dot(a, b):
    return jnp.dot(a, b, preferred_element_type=f32)


def dot_nt(a, b):
    return lax.dot_general(a, b, (((1,), (1,)), ((), ())), preferred_element_type=f32)


def dot_tn(a, b):
    return lax.dot_general(a, b, (((0,), (0,)), ((), ())), preferred_element_type=f32)


def inverse_rms(v):
    return lax.rsqrt(jnp.mean(v * v, axis=-1, keepdims=True) + EPS)


def norm_back(v, r, g, e):
    ev = e * v
    inner = jnp.mean(g * ev, axis=-1, keepdims=True)
    gain_axes = tuple(range(v.ndim - 1))
    return r * (g * e) - v * (r * r * r * inner), jnp.sum(ev * r, axis=gain_axes)


def rotary(v, cosine, sine):
    former, latter = v[..., :128], v[..., 128:]
    return jnp.concatenate([former * cosine - latter * sine, latter * cosine + former * sine], axis=-1)


def gelu_tanh(v):
    return 0.5 * v * (1.0 + jnp.tanh(0.7978845608028654 * (v + 0.044715 * v * v * v)))


def gated_hidden(gate_in, up_in):
    return gelu_tanh(gate_in) * up_in


def per_device(
    tokens,
    grad_out,
    attn_pre_gain,
    w_query,
    query_gain,
    key_gain,
    w_keyval,
    w_out,
    attn_post_gain,
    ffn_pre_gain,
    w_gate,
    w_up,
    w_down,
    ffn_post_gain,
):
    seq = lax.axis_index("seq")
    mp = lax.axis_index("mp")
    xl, z, y = seq // 16, seq // 4 % 4, seq % 4
    xh, c = mp // 2, mp % 2

    kv_mine = lax.dynamic_slice_in_dim(w_keyval, 256 * c, 256, 1)
    kv_other = fetch(lax.dynamic_slice_in_dim(w_keyval, 256 * (1 - c), 256, 1), c=1)
    kv18 = jnp.where(
        c == 0,
        jnp.concatenate([kv_mine, kv_other], axis=0),
        jnp.concatenate([kv_other, kv_mine], axis=0),
    )
    short = jnp.pad(jnp.stack([query_gain, key_gain], axis=1), ((0, 28), (0, 0)))
    gains = jnp.stack([attn_pre_gain, attn_post_gain, ffn_pre_gain, ffn_post_gain], axis=1)
    gains = jnp.pad(jnp.concatenate([gains, short], axis=1), ((0, 0), (0, 122)))
    parcel = jnp.concatenate([w_query, gains, w_out.T, kv18.reshape(36, 128)], axis=1)
    parcels = [
        [parcel, fetch(parcel, xh=1)],
        [fetch(parcel, xl=1), fetch(parcel, xl=1, xh=1)],
    ]

    def kv36(pair):
        own, far = pair[0][:, 640:].reshape(18, 256), pair[1][:, 640:].reshape(18, 256)
        return jnp.where(
            xh == 0, jnp.concatenate([own, far], axis=0), jnp.concatenate([far, own], axis=0)
        )

    block_a = jnp.concatenate(
        [jnp.concatenate([p[0][:, :256], p[1][:, :256], p[0][:, 256:384]], axis=1) for p in parcels],
        axis=0,
    )
    block_b = jnp.concatenate(
        [jnp.concatenate([kv36(p), p[0][:, 384:640], p[1][:, 384:640]], axis=1) for p in parcels],
        axis=0,
    )
    part_a = gather_grid(block_a, 0, False)
    part_b = gather_grid(block_b, 1, False)
    part_ao = fetch(part_a[:, :512], c=1)
    part_bo = fetch(part_b, c=1)

    ffn_own = jnp.stack([w_gate, w_up, w_down.T])
    ffn_pair = jnp.concatenate([ffn_own, fetch(ffn_own, xl=1)], axis=1)
    gate_weight = gather_grid(ffn_pair[0], 0, True)
    up_weight = gather_grid(ffn_pair[1], 1, True)
    down_a = gather_grid(ffn_pair[2][:, :CUT], 0, True)
    down_b = gather_grid(ffn_pair[2][:, CUT:], 1, True)

    half = fetch_line(lax.dynamic_slice_in_dim(tokens, 256 * c, 256, 0), -4)
    half_other = fetch(half, c=1)
    before = jnp.where(
        c == 0,
        jnp.concatenate([half, half_other], axis=0),
        jnp.concatenate([half_other, half], axis=0),
    )
    rows = lax.dynamic_slice_in_dim(jnp.concatenate([before, tokens], axis=0), ROWS * mp, KEYS, 0)
    column = jnp.arange(D, dtype=jnp.int32)
    zr, yr, xr, place = column // 288, column // 72 % 4, column // 36 % 2, column % 36
    owner = (xl ^ xr) * 16 + (z + zr) % 4 * 4 + (y + yr) % 4
    order = (column[:, None] == (owner * 36 + place)[None, :]).astype(bf16)
    short_owner = jnp.where(place < 8, owner * 8 + place, -1)
    short_order = (short_owner[:, None] == jnp.arange(HD, dtype=jnp.int32)[None, :]).astype(bf16)
    x_keys = dot(rows, order).astype(bf16).astype(f32)
    x = x_keys[WINDOW:]
    e_out = dot(lax.dynamic_slice_in_dim(grad_out, ROWS * mp, ROWS, 0), order).astype(bf16).astype(f32)
    r_keys = inverse_rms(x_keys)

    gain_cols = part_a[:, 512:]
    gain_rows = gain_cols[:, :8].T.astype(f32)
    pre_gain, post_gain, ffn_pre, ffn_post = (gain_rows[k : k + 1] for k in range(4))
    short_rows = dot_tn(gain_cols, short_order)
    qnorm_gain, knorm_gain = short_rows[4:5], short_rows[5:6]

    first_pos = seq % SEQ_BLOCKS * 512 + ROWS * mp
    positions = (first_pos - WINDOW + jnp.arange(KEYS, dtype=jnp.int32)).astype(f32)
    exponent = jnp.arange(HD // 2, dtype=f32) * (-2.0 / HD)
    angle = positions[:, None] * jnp.power(10000.0, exponent)[None, :]
    cosine, sine = jnp.cos(angle), jnp.sin(angle)
    cos_q, sin_q = cosine[WINDOW:], sine[WINDOW:]
    xn_keys = (x_keys * r_keys * pre_gain).astype(bf16)
    xn = xn_keys[WINDOW:]
    q_raw = [dot(xn, part_a[:, :512]), dot(xn, part_ao)]
    q_raw = jnp.stack([q_raw[h // 2][:, h % 2 * HD : h % 2 * HD + HD] for h in range(4)])
    kv_here, kv_there = dot(xn_keys, part_b[:, :HD]), dot(xn_keys, part_bo[:, :HD])
    key_raw = jnp.where(c == 0, kv_here, kv_there)
    values = jnp.where(c == 0, kv_there, kv_here).astype(bf16)
    r_q, r_k = inverse_rms(q_raw), inverse_rms(key_raw)
    query = rotary(q_raw * r_q * qnorm_gain, cos_q, sin_q).astype(bf16).reshape(4 * ROWS, HD)
    keys = rotary(key_raw * r_k * knorm_gain, cosine, sine).astype(bf16)
    row_ids = jnp.arange(ROWS, dtype=jnp.int32)[:, None]
    key_ids = jnp.arange(KEYS, dtype=jnp.int32)[None, :]
    allowed = (key_ids > row_ids) & (key_ids <= row_ids + WINDOW) & (key_ids + first_pos >= WINDOW)
    score = dot_nt(query, keys).reshape(4, ROWS, KEYS) * SCALE
    score = jnp.where(allowed[None], score, MASKED)
    peak = jnp.max(score, axis=-1, keepdims=True)
    weight = jnp.exp(score - peak)
    prob = weight / jnp.sum(weight, axis=-1, keepdims=True)
    prob_low = prob.astype(bf16).reshape(4 * ROWS, KEYS)
    att = dot(prob_low, values).astype(bf16).reshape(4, ROWS, HD)
    att = jnp.concatenate([att[h] for h in range(4)], axis=1)
    out_own, out_other = part_b[:, HD:], part_bo[:, HD:]
    branch = dot_nt(att[:, :512], out_own) + dot_nt(att[:, 512:], out_other)
    r_branch = inverse_rms(branch)
    mid = x + branch * r_branch * post_gain
    r_mid = inverse_rms(mid)
    hn_rows = (mid * r_mid * ffn_pre).astype(bf16)

    hn = gather_rows(hn_rows)
    gate = dot(hn, gate_weight)
    up = dot(hn, up_weight)
    hidden = gated_hidden(gate, up).astype(bf16)
    hidden_a, hidden_b = hidden[:, :CUT], hidden[:, CUT:]
    ffn = scatter_rows((dot_nt(hidden_a, down_a) + dot_nt(hidden_b, down_b)).astype(bf16))
    r_ffn = inverse_rms(ffn)
    output_rows = (mid + ffn * r_ffn * ffn_post).astype(bf16)
    d_ffn_rows, grad_ffn_post = norm_back(ffn, r_ffn, ffn_post, e_out)
    d_ffn = gather_rows(d_ffn_rows.astype(bf16))
    d_hidden = jnp.concatenate([dot(d_ffn, down_a), dot(d_ffn, down_b)], axis=1)
    _, gate_pull = jax.vjp(gated_hidden, gate, up)
    d_gate, d_up = gate_pull(d_hidden)
    d_gate, d_up = d_gate.astype(bf16), d_up.astype(bf16)
    d_hn = scatter_rows((dot_nt(d_gate, gate_weight) + dot_nt(d_up, up_weight)).astype(bf16))
    g_down_a = scatter_grid(dot_tn(d_ffn, hidden_a).astype(bf16), 0, True)
    g_down_b = scatter_grid(dot_tn(d_ffn, hidden_b).astype(bf16), 1, True)
    g_gate = scatter_grid(dot_tn(hn, d_gate).astype(bf16), 0, True)
    g_up = scatter_grid(dot_tn(hn, d_up).astype(bf16), 1, True)
    g_ffn = jnp.stack([g_gate, g_up, jnp.concatenate([g_down_a, g_down_b], axis=1)])
    g_ffn = add(g_ffn[:, :36], fetch(g_ffn[:, 36:].astype(bf16), xl=1))

    d_mid, grad_ffn_pre = norm_back(mid, r_mid, ffn_pre, d_hn)
    d_mid = d_mid + e_out
    d_branch, grad_post = norm_back(branch, r_branch, post_gain, d_mid)
    d_branch = d_branch.astype(bf16)
    d_att = [dot(d_branch, out_own), dot(d_branch, out_other)]
    d_att = jnp.stack([d_att[h // 2][:, h % 2 * HD : h % 2 * HD + HD] for h in range(4)])
    d_att = d_att.astype(bf16).reshape(4 * ROWS, HD)
    d_prob = dot_nt(d_att, values).reshape(4, ROWS, KEYS)
    delta = jnp.sum(prob * d_prob, axis=-1, keepdims=True)
    d_score = (prob * (d_prob - delta)).astype(bf16).reshape(4 * ROWS, KEYS)
    d_query = dot(d_score, keys).reshape(4, ROWS, HD) * SCALE
    d_kv = jnp.concatenate(
        [dot_tn(d_score, query) * SCALE, dot_tn(prob_low, d_att)], axis=1
    ).reshape(5, ROWS, 2 * HD)
    d_kv_low = d_kv[:4].astype(bf16)
    d_kv = add(d_kv[4], *[fetch_line(d_kv_low[k], 4 - k) for k in range(4)])
    d_key = rotary(d_kv[:, :HD], cos_q, -sin_q)
    d_key_raw, grad_key_gain = norm_back(key_raw[WINDOW:], r_k[WINDOW:], knorm_gain, d_key)
    d_key_raw = d_key_raw.astype(bf16)
    d_value = d_kv[:, HD:].astype(bf16)
    d_here = jnp.where(c == 0, d_key_raw, d_value)
    d_there = jnp.where(c == 0, d_value, d_key_raw)
    d_q_raw, grad_query_gain = norm_back(q_raw, r_q, qnorm_gain, rotary(d_query, cos_q, -sin_q))
    d_q_raw = d_q_raw.astype(bf16)
    d_q_own = jnp.concatenate([d_q_raw[0], d_q_raw[1]], axis=1)
    d_q_other = jnp.concatenate([d_q_raw[2], d_q_raw[3]], axis=1)
    d_xn = (
        dot_nt(d_q_own, part_a[:, :512])
        + dot_nt(d_q_other, part_ao)
        + dot_nt(d_here, part_b[:, :HD])
        + dot_nt(d_there, part_bo[:, :HD])
    )
    d_x, grad_pre = norm_back(x, r_keys[WINDOW:], pre_gain, d_xn)
    d_tokens = (d_mid + d_x).astype(bf16)

    def finished(values_low):
        return in_order(gather_rows(dot_nt(values_low, order).astype(bf16)), xh, c)

    output = finished(output_rows)
    grad_tokens = finished(d_tokens)

    short_grads = dot_nt(jnp.stack([grad_query_gain, grad_key_gain]).astype(bf16), short_order)
    gain_grads = jnp.concatenate(
        [jnp.stack([grad_pre, grad_post, grad_ffn_pre, grad_ffn_post]), short_grads]
    )
    gain_grads = jnp.pad(gain_grads, ((0, 2), (0, 0))).T.astype(bf16)
    gain_grads = jnp.pad(gain_grads, ((0, 0), (0, 120)))
    own_a = jnp.concatenate([dot_tn(xn, d_q_own).astype(bf16), gain_grads], axis=1)
    other_a = jnp.concatenate([dot_tn(xn, d_q_other).astype(bf16), gain_grads], axis=1)
    own_b = jnp.concatenate([dot_tn(xn, d_here), dot_tn(d_branch, att[:, :512])], axis=1)
    other_b = jnp.concatenate([dot_tn(xn, d_there), dot_tn(d_branch, att[:, 512:])], axis=1)
    sum_a = add(own_a, fetch(other_a, c=1)).astype(bf16)
    sum_b = add(own_b, fetch(other_b.astype(bf16), c=1)).astype(bf16)
    sum_a = scatter_grid(sum_a, 0, False).astype(bf16)
    sum_b = scatter_grid(sum_b, 1, False).astype(bf16)

    def parcel_back(xr_, xhr):
        a, b = sum_a[36 * xr_ : 36 * xr_ + 36], sum_b[36 * xr_ : 36 * xr_ + 36]
        kv = jnp.where(xh ^ xhr == 0, b[:18, :HD], b[18:, :HD]).reshape(36, 128)
        return jnp.concatenate(
            [a[:, 256 * xhr : 256 * xhr + 256], a[:, 512:], b[:, 256 + 256 * xhr : 512 + 256 * xhr], kv],
            axis=1,
        )

    total = add(
        parcel_back(0, 0),
        fetch(parcel_back(0, 1), xh=1),
        fetch(parcel_back(1, 0), xl=1),
        fetch(parcel_back(1, 1), xl=1, xh=1),
    )
    g_kv = total[:, 640:].reshape(18, 256)
    g_kv_here = jnp.where(c == 0, g_kv[:9], g_kv[9:])
    g_kv_away = fetch(jnp.where(c == 0, g_kv[9:], g_kv[:9]).astype(bf16), c=1).astype(f32)
    g_keyval = jnp.where(
        c == 0,
        jnp.concatenate([g_kv_here, g_kv_away], axis=1),
        jnp.concatenate([g_kv_away, g_kv_here], axis=1),
    )
    g_gains = total[:, 256:264].T
    return (
        output,
        grad_tokens,
        g_gains[0],
        total[:, :256],
        g_gains[4, :8],
        g_gains[5, :8],
        g_keyval,
        total[:, 384:640].T,
        g_gains[1],
        g_gains[2],
        g_ffn[0],
        g_ffn[1],
        g_ffn[2].T,
        g_gains[3],
    )


def solution(mesh):
    row, vector, weight, weight_t = P("seq", None), P("seq"), P("seq", "mp"), P("mp", "seq")
    keyval = P(("seq", "mp"), None)
    return jax.shard_map(
        per_device,
        mesh=mesh,
        in_specs=(row, row, vector, weight, vector, vector, keyval, weight_t)
        + (vector, vector, weight, weight, weight_t, vector),
        out_specs=(row, row, vector, weight, vector, vector, keyval, weight_t)
        + (vector, vector, weight, weight, weight_t, vector),
        check_vma=False,
    )
```

time: 1650 us -> 588 us (0.36)
  blocking collectives: 634 us -> 0 us
  waiting for transfers between devices: 703 us -> 196 us
  starting transfers between devices: 80.5 us -> 178 us
  local copies, waits for them, and re-layouts: 75.8 us -> 54.3 us
  between operations: 21 us -> 3.57 us
    unnamed x3 -> x0, blocking collectives: 452 us -> none
    all_gather x4 -> x0, waiting for transfers between devices: 377 us -> none  [the longest x1 153 us: per_device(): lax.all_gather(w_up, 'seq', axis=0, tiled=True)]
    psum x4 -> x0, waiting for transfers between devices: 257 us -> none  [the longest x1 129 us: per_device(): branch = lax.psum(branch_part, 'mp')]
    ppermute x4 -> x118, waiting for transfers between devices: 13.3 us -> 196 us  [the longest x113 192 us: fetch(): return lax.ppermute(x, ('seq', 'mp'), pairs)]
    ppermute x4 -> x118, starting transfers between devices: 6.08 us -> 178 us  [the longest x113 167 us: fetch(): return lax.ppermute(x, ('seq', 'mp'), pairs)]
    all_gather x2 -> x0, blocking collectives: 137 us -> none  [the longest x1 71.7 us: per_device(): lax.all_gather(w_out, 'seq', axis=1, tiled=True)]
    unnamed x23 -> x0, starting transfers between devices: 73.4 us -> none
    unnamed x236 -> x295, local copies, waits for them, and re-layouts: 73.9 us -> 15.7 us
  transfers between devices with their start and end apart: 35 -> 118, of which waited for: 15 -> 52; matrix products, arithmetic and copies ran while one was open for 19% -> 25% of each run, Pallas kernels for 0% -> 0%
where the time goes in v1:
time: 588 us; the launch traced here: 577 us
  waiting for transfers between devices  196 us (33%)
  starting transfers between devices  178 us (30%)
  other arithmetic  74.7 us (13%)
  matrix products  70.1 us (12%)
  local copies, waits for them, and re-layouts  54.3 us (9%)
    ppermute x113, waiting for transfers between devices, fetch(): return lax.ppermute(x, ('seq', 'mp'), pairs)  192 us
    ppermute x113, starting transfers between devices, fetch(): return lax.ppermute(x, ('seq', 'mp'), pairs)  167 us
    dot_general x14, matrix products, dot(): return jnp.dot(a, b, preferred_element_type=f32)  24 us
    dot_general x13, matrix products, dot_tn(): lax.dot_general(a, b, (((0,), (0,)), ((), ())), preferred_element_type=f32)  22.9 us
    dot_general x14, matrix products, dot_nt(): lax.dot_general(a, b, (((1,), (1,)), ((), ())), preferred_element_type=f32)  20.4 us
    unnamed x295, local copies, waits for them, and re-layouts  15.7 us
  transfers between devices with their start and end apart: 118, of which 52 were waited for; matrix products, arithmetic and copies ran while one was open for 25% of the time, Pallas kernels for 0%

profile of v1, /device:TPU:1, one launch (start us, length us, event | category | flops | bytes accessed | tf_op | source)
XLA Modules:
  0.0 576.9 jit_solution(1467963404921431744)
XLA Ops:
  48.1 4.7 collective-permute-done.47
  70.8 7.9 %collective-permute-start.25 = (bf16[72,1728]{1,0:T(8,128)(2,1)S(1)}, bf16[72,1728]{1,0:T(8,128)(2,1)S(1)}, u32[]{:S(2)}, u32[]{:S(2)}) collective-permute-start(bf16[72,1728]{1,0:T(8,128)(2,1)S(1)} %get-tuple-element.96), channel_id=1, source_target_pairs={{32,0},{33,1},{34,2},{35,3},{36,4},{37,5},{38,6},{39,7},{40,8},{41... | collective-permute-start | bytes 746504 | tf_op jit(solution)/shard_map/ppermute | solution.py:38
  80.2 4.6 collective-permute-done.18
  90.9 8.6 %collective-permute-done.25 = bf16[72,1728]{1,0:T(8,128)(2,1)S(1)} collective-permute-done((bf16[72,1728]{1,0:T(8,128)(2,1)S(1)}, bf16[72,1728]{1,0:T(8,128)(2,1)S(1)}, u32[]{:S(2)}, u32[]{:S(2)}) %collective-permute-start.25) | collective-permute-done | bytes 248864 | tf_op jit(solution)/shard_map/ppermute | solution.py:38
  100.9 9.8 %collective-permute-start.1 = (bf16[256,1152]{1,0:T(8,128)(2,1)S(1)}, bf16[256,1152]{1,0:T(8,128)(2,1)S(1)}, u32[]{:S(2)}, u32[]{:S(2)}) collective-permute-start(bf16[256,1152]{1,0:T(8,128)(2,1)S(1)} %collective-permute-done), channel_id=1, source_target_pairs={{1,0},{0,1},{3,2},{2,3},{5,4},{4,5},{7,6},{6,7},{9,8},{8,9},{11,10... | collective-permute-start | bytes 1769480 | tf_op jit(solution)/shard_map/ppermute | solution.py:38
  114.8 9.6 %collective-permute-done.48 = bf16[4,72,832]{2,1,0:T(8,128)(2,1)S(1)} collective-permute-done((bf16[4,72,832]{2,1,0:T(8,128)(2,1)S(1)}, bf16[4,72,832]{2,1,0:T(8,128)(2,1)S(1)}, u32[]{:S(2)}, u32[]{:S(2)}) %collective-permute-start.48) | collective-permute-done | bytes 479264 | tf_op jit(solution)/shard_map/ppermute | solution.py:38
  137.6 15.6 %collective-permute-done.42 = bf16[2,72,896]{2,1,0:T(8,128)(2,1)S(1)} collective-permute-done((bf16[2,72,896]{2,1,0:T(8,128)(2,1)S(1)}, bf16[2,72,896]{2,1,0:T(8,128)(2,1)S(1)}, u32[]{:S(2)}, u32[]{:S(2)}) %collective-permute-start.42) | collective-permute-done | bytes 258080 | tf_op jit(solution)/shard_map/ppermute | solution.py:38
  164.7 14.1 %collective-permute-done.34 = bf16[4,72,1728]{2,1,0:T(8,128)(2,1)S(1)} collective-permute-done((bf16[4,72,1728]{2,1,0:T(8,128)(2,1)S(1)}, bf16[4,72,1728]{2,1,0:T(8,128)(2,1)S(1)}, u32[]{:S(2)}, u32[]{:S(2)}) %collective-permute-start.34) | collective-permute-done | bytes 995360 | tf_op jit(solution)/shard_map/ppermute | solution.py:38
  185.7 5.9 %collective-permute-done.30 = bf16[2,72,1728]{2,1,0:T(8,128)(2,1)S(1)} collective-permute-done((bf16[2,72,1728]{2,1,0:T(8,128)(2,1)S(1)}, bf16[2,72,1728]{2,1,0:T(8,128)(2,1)S(1)}, u32[]{:S(2)}, u32[]{:S(2)}) %collective-permute-start.30) | collective-permute-done | bytes 497696 | tf_op jit(solution)/shard_map/ppermute | solution.py:38
  228.2 6.2 %multiply_convert_fusion.1 = (bf16[512,1728]{0,1:T(8,128)(2,1)S(1)}, f32[512,1728]{0,1:T(8,128)}) fusion(f32[512,1728]{0,1:T(8,128)S(1)} %fusion.193, bf16[1152,1728]{1,0:T(8,128)(2,1)S(1)} %bitcast.421, bf16[128,1152]{1,0:T(8,128)(2,1)S(1)} %collective-permute-done.22, bf16[128,1152]{1,0:T(8,128)(2,1)S(1)} %collective-permute-done.21, ...), kind=kOutput, calls=%fused_computation.26 | convolution fusion | flops 2051997696 | bytes 14008320 | tf_op jit(solution)/shard_map/dot_general | solution.py:110
  242.0 9.5 %collective-permute-done.54 = bf16[128,1152]{1,0:T(8,128)(2,1)} collective-permute-done((bf16[128,1152]{1,0:T(8,128)(2,1)}, bf16[128,1152]{1,0:T(8,128)(2,1)}, u32[]{:S(2)}, u32[]{:S(2)}) %collective-permute-start.54) | collective-permute-done | bytes 294944 | tf_op jit(solution)/shard_map/ppermute | solution.py:38
  311.5 6.5 %copy.155 = bf16[1152,1728]{1,0:T(8,128)(2,1)} copy(bf16[1152,1728]{0,1:T(8,128)(2,1)} %convolution_convert_fusion) | data formatting | bytes 7962624 | tf_op jit(solution)/shard_map/convert_element_type | solution.py:284
  371.2 6.1 %collective-permute-start.67 = (bf16[128,512]{0,1:T(8,128)(2,1)S(1)}, bf16[128,512]{0,1:T(8,128)(2,1)S(1)}, u32[]{:S(2)}, u32[]{:S(2)}) collective-permute-start(bf16[128,512]{0,1:T(8,128)(2,1)S(1)} %get-tuple-element.103), channel_id=1, source_target_pairs={{1,0},{2,1},{3,2},{4,3},{5,4},{6,5},{7,6},{8,7},{9,8},{10,9},{11,1... | collective-permute-start | bytes 393224 | tf_op jit(solution)/shard_map/ppermute | solution.py:43
  384.0 4.9 collective-permute-start.104
  389.0 6.1 %collective-permute-start.97 = (bf16[4,72,1728]{2,1,0:T(8,128)(2,1)}, bf16[4,72,1728]{2,1,0:T(8,128)(2,1)}, u32[]{:S(2)}, u32[]{:S(2)}) collective-permute-start(bf16[4,72,1728]{2,1,0:T(8,128)(2,1)} %pad_maximum_fusion.18), channel_id=1, source_target_pairs={{48,0},{49,1},{50,2},{51,3},{52,4},{53,5},{54,6},{55,7},{56,8},{57... | collective-permute-start | bytes 2985992 | tf_op jit(solution)/shard_map/ppermute | solution.py:38
  418.5 4.6 collective-permute-start.69
  438.8 16.0 %collective-permute-done.99 = bf16[4,72,1728]{2,1,0:T(8,128)(2,1)S(1)} collective-permute-done((bf16[4,72,1728]{2,1,0:T(8,128)(2,1)S(1)}, bf16[4,72,1728]{2,1,0:T(8,128)(2,1)S(1)}, u32[]{:S(2)}, u32[]{:S(2)}) %collective-permute-start.99) | collective-permute-done | bytes 995360 | tf_op jit(solution)/shard_map/ppermute | solution.py:38
  477.0 6.8 %collective-permute-done.94 = bf16[72,1728]{1,0:T(8,128)(2,1)S(1)} collective-permute-done((bf16[72,1728]{1,0:T(8,128)(2,1)S(1)}, bf16[72,1728]{1,0:T(8,128)(2,1)S(1)}, u32[]{:S(2)}, u32[]{:S(2)}) %collective-permute-start.94) | collective-permute-done | bytes 248864 | tf_op jit(solution)/shard_map/ppermute | solution.py:38
  484.2 8.6 %collective-permute-start.117 = (bf16[3,36,1728]{2,1,0:T(8,128)(2,1)S(1)}, bf16[3,36,1728]{2,1,0:T(8,128)(2,1)S(1)}, u32[]{:S(2)}, u32[]{:S(2)}) collective-permute-start(bf16[3,36,1728]{2,1,0:T(8,128)(2,1)S(1)} %slice.1301), channel_id=1, source_target_pairs={{64,0},{65,1},{66,2},{67,3},{68,4},{69,5},{70,6},{71,7},{72,8},{73... | collective-permute-start | bytes 1119752 | tf_op jit(solution)/shard_map/ppermute | solution.py:38
  494.8 6.2 %collective-permute-done.117 = bf16[3,36,1728]{2,1,0:T(8,128)(2,1)S(1)} collective-permute-done((bf16[3,36,1728]{2,1,0:T(8,128)(2,1)S(1)}, bf16[3,36,1728]{2,1,0:T(8,128)(2,1)S(1)}, u32[]{:S(2)}, u32[]{:S(2)}) %collective-permute-start.117) | collective-permute-done | bytes 373280 | tf_op jit(solution)/shard_map/ppermute | solution.py:38
  513.4 11.9 %collective-permute-done.72 = bf16[4,72,640]{2,1,0:T(8,128)(2,1)S(1)} collective-permute-done((bf16[4,72,640]{2,1,0:T(8,128)(2,1)S(1)}, bf16[4,72,640]{2,1,0:T(8,128)(2,1)S(1)}, u32[]{:S(2)}, u32[]{:S(2)}) %collective-permute-start.72) | collective-permute-done | bytes 368672 | tf_op jit(solution)/shard_map/ppermute | solution.py:38
  534.2 5.9 %collective-permute-done.81 = bf16[4,72,768]{2,1,0:T(8,128)(2,1)S(1)} collective-permute-done((bf16[4,72,768]{2,1,0:T(8,128)(2,1)S(1)}, bf16[4,72,768]{2,1,0:T(8,128)(2,1)S(1)}, u32[]{:S(2)}, u32[]{:S(2)}) %collective-permute-start.81) | collective-permute-done | bytes 442400 | tf_op jit(solution)/shard_map/ppermute | solution.py:38
  542.4 9.0 %collective-permute-done.80 = bf16[4,72,768]{2,1,0:T(8,128)(2,1)S(1)} collective-permute-done((bf16[4,72,768]{2,1,0:T(8,128)(2,1)S(1)}, bf16[4,72,768]{2,1,0:T(8,128)(2,1)S(1)}, u32[]{:S(2)}, u32[]{:S(2)}) %collective-permute-start.80) | collective-permute-done | bytes 442400 | tf_op jit(solution)/shard_map/ppermute | solution.py:38
  566.8 7.8 %collective-permute-start.88 = (bf16[9,256]{1,0:T(8,128)(2,1)S(1)}, bf16[9,256]{1,0:T(8,128)(2,1)S(1)}, u32[]{:S(2)}, u32[]{:S(2)}) collective-permute-start(bf16[9,256]{1,0:T(8,128)(2,1)S(1)} %convert_element_type.581), channel_id=1, source_target_pairs={{1,0},{0,1},{3,2},{2,3},{5,4},{4,5},{7,6},{6,7},{9,8},{8,9},{11,10... | collective-permute-start | bytes 13832 | tf_op jit(solution)/shard_map/ppermute | solution.py:38
  (758 shorter events, 376.4 us)
Async XLA Ops:
  4.2 32.9 %collective-permute-start.23 = (bf16[3,36,1728]{2,1,0:T(8,128)(2,1)S(1)}, bf16[3,36,1728]{2,1,0:T(8,128)(2,1)S(1)}, u32[]{:S(2)}, u32[]{:S(2)}) collective-permute-start(bf16[3,36,1728]{2,1,0:T(8,128)(2,1)S(1)} %pad_maximum_fusion.30), channel_id=1, source_target_pairs={{64,0},{65,1},{66,2},{67,3},{68,4},{69,5},{70,6},{71,7},{72,8},{73... | collective-permute-start | bytes 1119752 | tf_op jit(solution)/shard_map/ppermute | solution.py:38
  70.8 28.6 %collective-permute-start.25 = (bf16[72,1728]{1,0:T(8,128)(2,1)S(1)}, bf16[72,1728]{1,0:T(8,128)(2,1)S(1)}, u32[]{:S(2)}, u32[]{:S(2)}) collective-permute-start(bf16[72,1728]{1,0:T(8,128)(2,1)S(1)} %get-tuple-element.96), channel_id=1, source_target_pairs={{32,0},{33,1},{34,2},{35,3},{36,4},{37,5},{38,6},{39,7},{40,8},{41... | collective-permute-start | bytes 746504 | tf_op jit(solution)/shard_map/ppermute | solution.py:38
  99.4 26.9 %collective-permute-start.41 = (bf16[4,72,896]{2,1,0:T(8,128)(2,1)S(1)}, bf16[4,72,896]{2,1,0:T(8,128)(2,1)S(1)}, u32[]{:S(2)}, u32[]{:S(2)}) collective-permute-start(bf16[4,72,896]{2,1,0:T(8,128)(2,1)S(1)} %get-tuple-element.117), channel_id=1, source_target_pairs={{4,0},{5,1},{6,2},{7,3},{8,4},{9,5},{10,6},{11,7},{12,8},{13,9},{1... | collective-permute-start | bytes 1548296 | tf_op jit(solution)/shard_map/ppermute | solution.py:38
  99.4 28.8 %collective-permute-start.43 = (bf16[4,72,896]{2,1,0:T(8,128)(2,1)S(1)}, bf16[4,72,896]{2,1,0:T(8,128)(2,1)S(1)}, u32[]{:S(2)}, u32[]{:S(2)}) collective-permute-start(bf16[4,72,896]{2,1,0:T(8,128)(2,1)S(1)} %get-tuple-element.117), channel_id=1, source_target_pairs={{12,0},{13,1},{14,2},{15,3},{0,4},{1,5},{2,6},{3,7},{4,8},{5,9},{6... | collective-permute-start | bytes 1548296 | tf_op jit(solution)/shard_map/ppermute | solution.py:38
  100.9 27.4 %collective-permute-start.1 = (bf16[256,1152]{1,0:T(8,128)(2,1)S(1)}, bf16[256,1152]{1,0:T(8,128)(2,1)S(1)}, u32[]{:S(2)}, u32[]{:S(2)}) collective-permute-start(bf16[256,1152]{1,0:T(8,128)(2,1)S(1)} %collective-permute-done), channel_id=1, source_target_pairs={{1,0},{0,1},{3,2},{2,3},{5,4},{4,5},{7,6},{6,7},{9,8},{8,9},{11,10... | collective-permute-start | bytes 1769480 | tf_op jit(solution)/shard_map/ppermute | solution.py:38
  124.4 59.8 %collective-permute-start.12 = (bf16[1152,512]{1,0:T(8,128)(2,1)S(1)}, bf16[1152,512]{1,0:T(8,128)(2,1)S(1)}, u32[]{:S(2)}, u32[]{:S(2)}) collective-permute-start(bf16[1152,512]{1,0:T(8,128)(2,1)S(1)} %slice.902), channel_id=1, source_target_pairs={{1,0},{0,1},{3,2},{2,3},{5,4},{4,5},{7,6},{6,7},{9,8},{8,9},{11,10... | collective-permute-start | bytes 3538952 | tf_op jit(solution)/shard_map/ppermute | solution.py:38
  125.3 32.6 %collective-permute-start.27 = (bf16[4,72,1728]{2,1,0:T(8,128)(2,1)S(1)}, bf16[4,72,1728]{2,1,0:T(8,128)(2,1)S(1)}, u32[]{:S(2)}, u32[]{:S(2)}) collective-permute-start(bf16[4,72,1728]{2,1,0:T(8,128)(2,1)S(1)} %get-tuple-element.87), channel_id=1, source_target_pairs={{4,0},{5,1},{6,2},{7,3},{8,4},{9,5},{10,6},{11,7},{12,8},{13,9},{1... | collective-permute-start | bytes 2985992 | tf_op jit(solution)/shard_map/ppermute | solution.py:38
  136.7 26.3 %collective-permute-start.29 = (bf16[4,72,1728]{2,1,0:T(8,128)(2,1)S(1)}, bf16[4,72,1728]{2,1,0:T(8,128)(2,1)S(1)}, u32[]{:S(2)}, u32[]{:S(2)}) collective-permute-start(bf16[4,72,1728]{2,1,0:T(8,128)(2,1)S(1)} %get-tuple-element.87), channel_id=1, source_target_pairs={{12,0},{13,1},{14,2},{15,3},{0,4},{1,5},{2,6},{3,7},{4,8},{5,9},{6... | collective-permute-start | bytes 2985992 | tf_op jit(solution)/shard_map/ppermute | solution.py:38
  157.8 34.9 %collective-permute-start.19 = (bf16[1152,768]{1,0:T(8,128)(2,1)S(1)}, bf16[1152,768]{1,0:T(8,128)(2,1)S(1)}, u32[]{:S(2)}, u32[]{:S(2)}) collective-permute-start(bf16[1152,768]{1,0:T(8,128)(2,1)S(1)} %bitcast.409), channel_id=1, source_target_pairs={{1,0},{0,1},{3,2},{2,3},{5,4},{4,5},{7,6},{6,7},{9,8},{8,9},{11,10... | collective-permute-start | bytes 5308424 | tf_op jit(solution)/shard_map/ppermute | solution.py:38
  181.9 32.9 %collective-permute-start.35 = (bf16[2,72,1728]{2,1,0:T(8,128)(2,1)}, bf16[2,72,1728]{2,1,0:T(8,128)(2,1)}, u32[]{:S(2)}, u32[]{:S(2)}) collective-permute-start(bf16[2,72,1728]{2,1,0:T(8,128)(2,1)} %slice.936), channel_id=1, source_target_pairs={{16,0},{17,1},{18,2},{19,3},{20,4},{21,5},{22,6},{23,7},{24,8},{25... | collective-permute-start | bytes 1493000 | tf_op jit(solution)/shard_map/ppermute | solution.py:38
  184.2 30.6 %collective-permute-start.37 = (bf16[2,72,1728]{2,1,0:T(8,128)(2,1)}, bf16[2,72,1728]{2,1,0:T(8,128)(2,1)}, u32[]{:S(2)}, u32[]{:S(2)}) collective-permute-start(bf16[2,72,1728]{2,1,0:T(8,128)(2,1)} %slice.937), channel_id=1, source_target_pairs={{48,0},{49,1},{50,2},{51,3},{52,4},{53,5},{54,6},{55,7},{56,8},{57... | collective-permute-start | bytes 1493000 | tf_op jit(solution)/shard_map/ppermute | solution.py:38
  294.8 63.0 %collective-permute-start.61 = (bf16[128,1152]{1,0:T(8,128)(2,1)}, bf16[128,1152]{1,0:T(8,128)(2,1)}, u32[]{:S(2)}, u32[]{:S(2)}) collective-permute-start(bf16[128,1152]{1,0:T(8,128)(2,1)} %get-tuple-element.76), channel_id=1, source_target_pairs={{1,0},{0,1},{3,2},{2,3},{5,4},{4,5},{7,6},{6,7},{9,8},{8,9},{11,10... | collective-permute-start | bytes 884744 | tf_op jit(solution)/shard_map/ppermute | solution.py:38
  298.6 28.7 %collective-permute-start.112 = (bf16[2,72,832]{2,1,0:T(8,128)(2,1)}, bf16[2,72,832]{2,1,0:T(8,128)(2,1)}, u32[]{:S(2)}, u32[]{:S(2)}) collective-permute-start(bf16[2,72,832]{2,1,0:T(8,128)(2,1)} %bitcast.166), channel_id=1, source_target_pairs={{16,0},{17,1},{18,2},{19,3},{20,4},{21,5},{22,6},{23,7},{24,8},{25... | collective-permute-start | bytes 718856 | tf_op jit(solution)/shard_map/ppermute | solution.py:38
  302.1 29.3 %collective-permute-start.110 = (bf16[2,72,832]{2,1,0:T(8,128)(2,1)}, bf16[2,72,832]{2,1,0:T(8,128)(2,1)}, u32[]{:S(2)}, u32[]{:S(2)}) collective-permute-start(bf16[2,72,832]{2,1,0:T(8,128)(2,1)} %bitcast.162), channel_id=1, source_target_pairs={{48,0},{49,1},{50,2},{51,3},{52,4},{53,5},{54,6},{55,7},{56,8},{57... | collective-permute-start | bytes 718856 | tf_op jit(solution)/shard_map/ppermute | solution.py:38
  307.1 28.5 %collective-permute-start.103 = (bf16[2,72,896]{2,1,0:T(8,128)(2,1)}, bf16[2,72,896]{2,1,0:T(8,128)(2,1)}, u32[]{:S(2)}, u32[]{:S(2)}) collective-permute-start(bf16[2,72,896]{2,1,0:T(8,128)(2,1)} %get-tuple-element.59), channel_id=1, source_target_pairs={{12,0},{13,1},{14,2},{15,3},{0,4},{1,5},{2,6},{3,7},{4,8},{5,9},{6... | collective-permute-start | bytes 774152 | tf_op jit(solution)/shard_map/ppermute | solution.py:38
  345.1 35.3 %collective-permute-start.111 = (bf16[4,72,832]{2,1,0:T(8,128)(2,1)S(1)}, bf16[4,72,832]{2,1,0:T(8,128)(2,1)S(1)}, u32[]{:S(2)}, u32[]{:S(2)}) collective-permute-start(bf16[4,72,832]{2,1,0:T(8,128)(2,1)S(1)} %pad_maximum_fusion.27), channel_id=1, source_target_pairs={{48,0},{49,1},{50,2},{51,3},{52,4},{53,5},{54,6},{55,7},{56,8},{57... | collective-permute-start | bytes 1437704 | tf_op jit(solution)/shard_map/ppermute | solution.py:38
  349.5 32.2 %collective-permute-start.113 = (bf16[4,72,832]{2,1,0:T(8,128)(2,1)S(1)}, bf16[4,72,832]{2,1,0:T(8,128)(2,1)S(1)}, u32[]{:S(2)}, u32[]{:S(2)}) collective-permute-start(bf16[4,72,832]{2,1,0:T(8,128)(2,1)S(1)} %pad_maximum_fusion.28), channel_id=1, source_target_pairs={{16,0},{17,1},{18,2},{19,3},{20,4},{21,5},{22,6},{23,7},{24,8},{25... | collective-permute-start | bytes 1437704 | tf_op jit(solution)/shard_map/ppermute | solution.py:38
  351.8 66.2 %collective-permute-start.106 = (bf16[4,72,896]{2,1,0:T(8,128)(2,1)}, bf16[4,72,896]{2,1,0:T(8,128)(2,1)}, u32[]{:S(2)}, u32[]{:S(2)}) collective-permute-start(bf16[4,72,896]{2,1,0:T(8,128)(2,1)} %pad_maximum_fusion.26), channel_id=1, source_target_pairs={{4,0},{5,1},{6,2},{7,3},{8,4},{9,5},{10,6},{11,7},{12,8},{13,9},{1... | collective-permute-start | bytes 1548296 | tf_op jit(solution)/shard_map/ppermute | solution.py:38
  384.0 34.4 %collective-permute-start.104 = (bf16[4,72,896]{2,1,0:T(8,128)(2,1)}, bf16[4,72,896]{2,1,0:T(8,128)(2,1)}, u32[]{:S(2)}, u32[]{:S(2)}) collective-permute-start(bf16[4,72,896]{2,1,0:T(8,128)(2,1)} %pad_maximum_fusion.25), channel_id=1, source_target_pairs={{12,0},{13,1},{14,2},{15,3},{0,4},{1,5},{2,6},{3,7},{4,8},{5,9},{6... | collective-permute-start | bytes 1548296 | tf_op jit(solution)/shard_map/ppermute | solution.py:38
  389.0 49.7 %collective-permute-start.97 = (bf16[4,72,1728]{2,1,0:T(8,128)(2,1)}, bf16[4,72,1728]{2,1,0:T(8,128)(2,1)}, u32[]{:S(2)}, u32[]{:S(2)}) collective-permute-start(bf16[4,72,1728]{2,1,0:T(8,128)(2,1)} %pad_maximum_fusion.18), channel_id=1, source_target_pairs={{48,0},{49,1},{50,2},{51,3},{52,4},{53,5},{54,6},{55,7},{56,8},{57... | collective-permute-start | bytes 2985992 | tf_op jit(solution)/shard_map/ppermute | solution.py:38
  395.1 29.5 %collective-permute-start.114 = (bf16[72,832]{1,0:T(8,128)(2,1)}, bf16[72,832]{1,0:T(8,128)(2,1)}, u32[]{:S(2)}, u32[]{:S(2)}) collective-permute-start(bf16[72,832]{1,0:T(8,128)(2,1)} %get-tuple-element.113), channel_id=1, source_target_pairs={{12,0},{13,1},{14,2},{15,3},{0,4},{1,5},{2,6},{3,7},{4,8},{5,9},{6... | collective-permute-start | bytes 359432 | tf_op jit(solution)/shard_map/ppermute | solution.py:38
  395.2 29.5 %collective-permute-start.116 = (bf16[72,832]{1,0:T(8,128)(2,1)}, bf16[72,832]{1,0:T(8,128)(2,1)}, u32[]{:S(2)}, u32[]{:S(2)}) collective-permute-start(bf16[72,832]{1,0:T(8,128)(2,1)} %get-tuple-element.114), channel_id=1, source_target_pairs={{4,0},{5,1},{6,2},{7,3},{8,4},{9,5},{10,6},{11,7},{12,8},{13,9},{1... | collective-permute-start | bytes 359432 | tf_op jit(solution)/shard_map/ppermute | solution.py:38
  437.7 64.2 %collective-permute-start.71 = (bf16[1152,640]{0,1:T(8,128)(2,1)S(1)}, bf16[1152,640]{0,1:T(8,128)(2,1)S(1)}, u32[]{:S(2)}, u32[]{:S(2)}) collective-permute-start(bf16[1152,640]{0,1:T(8,128)(2,1)S(1)} %fusion.32), channel_id=1, source_target_pairs={{1,0},{0,1},{3,2},{2,3},{5,4},{4,5},{7,6},{6,7},{9,8},{8,9},{11,10... | collective-permute-start | bytes 4423688 | tf_op jit(solution)/shard_map/ppermute | solution.py:38
  438.7 72.7 %collective-permute-start.78 = (bf16[1152,768]{1,0:T(8,128)(2,1)}, bf16[1152,768]{1,0:T(8,128)(2,1)}, u32[]{:S(2)}, u32[]{:S(2)}) collective-permute-start(bf16[1152,768]{1,0:T(8,128)(2,1)} %pad_maximum_fusion.6), channel_id=1, source_target_pairs={{1,0},{0,1},{3,2},{2,3},{5,4},{4,5},{7,6},{6,7},{9,8},{8,9},{11,10... | collective-permute-start | bytes 5308424 | tf_op jit(solution)/shard_map/ppermute | solution.py:38
  (243 other events, 2559.0 us)
